TPU v7x, 1024 devices: a whole 4x4x32 slice. The times are simulated.
1024 devices in a mesh: src: 4 (over x), space: 256 (over y, z, core).
Axes of the slice: x: 4, y: 4, z: 32, core: 2. Of those that a mesh axis runs over, the one named last changes fastest.
Arguments:
- adjoint_source: float32 [4, 6, 1024, 64, 128], P('src', None, 'space'), may hold values from -6 to 6
- forward_field: bfloat16 [4, 6, 1024, 64, 128], P('src', None, 'space'), may hold values from -6 to 6
- medium: float32 [2, 1024, 64, 128], P(None, 'space'), may hold values from 0.3 to 3
- plane_map: int32 [1024, 64], P('space'), may hold values from 0 to 255, as said below
- depth: int32 [4, 1024, 64], P('src', 'space'), may hold values from 1 to 128
- rough: float32 [9, 256, 32, 128], P(None, 'space'), may hold values from 0.2 to 1
Outputs:
- gradient: float32 [256, 32, 128], P('space')
Inputs may be any that keep to these rules, and one draw needn't show every extreme that they name: plane_map[x, y] differs from x // 4 by at most 2.
All inputs are finite; a program needn't handle non-finite values.
Results may differ from a plain program's by a relative error of at most 0.0003.
Values sent between devices are 32-bit elements; how exact they have to be, the bound alone decides.
A program may use at most 32 MiB of HBM per device.

v0:
```python
import jax
import jax.numpy as jnp
from jax import lax
from jax.sharding import PartitionSpec as P

SWEEPS = 4
REACH = 2


sweep_steps = (0.323, 1.658, 0.422, 0.752)


def padded_2(shard, sides, width):
    for axis, dim in sides:
        size, length = (lax.axis_size(axis), shard.shape[dim])
        up = [(i, (i + 1) % size) for i in range(size - 1)]
        down = [(j, i) for i, j in up]
        last = lax.slice_in_dim(shard, length - width, length, axis=dim)
        first = lax.slice_in_dim(shard, 0, width, axis=dim)
        before = lax.ppermute(last, axis, up)
        after = lax.ppermute(first, axis, down)
        shard = jnp.concatenate([before, shard, after], axis=dim)
    return shard


def shifted(value, axis, steps):
    count = lax.axis_size(axis)
    first, last = (max(0, -steps), min(count, count - steps))
    return lax.ppermute(value, axis, [(source, source + steps) for source in range(first, last)])


def from_everyone(shard, axis):
    copies = jnp.broadcast_to(shard, (lax.axis_size(axis), *shard.shape))
    return lax.all_to_all(copies, axis, split_axis=0, concat_axis=0, tiled=True)


def over_copies(shard, axis):
    everything = from_everyone(shard, axis)
    return jnp.sum(everything, axis=0)


def ahead_rows(value):
    return jnp.concatenate([value[..., 1:, :], jnp.zeros_like(value[..., :1, :])], axis=-2)


def ahead_depth(value):
    return jnp.concatenate([value[..., 1:], jnp.zeros_like(value[..., :1])], axis=-1)


def behind_rows(value):
    return jnp.concatenate([jnp.zeros_like(value[..., :1, :]), value[..., :-1, :]], axis=-2) - value


def behind_depth(value):
    return jnp.concatenate([jnp.zeros_like(value[..., :1]), value[..., :-1]], axis=-1) - value


def lower_planes(value):
    return value[..., :-1, :, :]


def upper_planes(value):
    return value[..., 1:, :, :]


def step_planes(value):
    return value[..., 1:, :, :] - value[..., :-1, :, :]


def back_planes(value):
    return value[..., :-1, :, :] - value[..., 1:, :, :]


def curl_curl(padded, inside):
    shape = padded.shape
    planes = shape[-3]
    split = padded.reshape(shape[:-4] + (2, 3) + shape[-3:])
    field_x = split[..., 0, :, :, :]
    field_y = split[..., 1, :, :, :]
    field_z = split[..., 2, :, :, :]
    front = inside[:-1][:, None, None]
    curl_x = (
        ahead_rows(lower_planes(field_z))
        - lower_planes(field_z)
        - (ahead_depth(lower_planes(field_y)) - lower_planes(field_y))
    )
    curl_y = ahead_depth(lower_planes(field_x)) - lower_planes(field_x) - step_planes(field_z)
    curl_z = step_planes(field_y) - (ahead_rows(lower_planes(field_x)) - lower_planes(field_x))
    curl_x = curl_x * front
    curl_y = curl_y * front
    curl_z = curl_z * front
    out_x = behind_depth(upper_planes(curl_y)) - behind_rows(upper_planes(curl_z))
    out_y = back_planes(curl_z) - behind_depth(upper_planes(curl_x))
    out_z = behind_rows(upper_planes(curl_x)) - back_planes(curl_y)
    stacked = jnp.stack([out_x, out_y, out_z], axis=-4)
    return stacked.reshape(shape[:-4] + (6, planes - 2) + shape[-2:])


def sweep(padded, source, mass_real, mass_imag, inside, weight):
    image = curl_curl(padded, inside)
    center = padded[..., 1:-1, :, :]
    real_part = center[..., 0:3, :, :, :]
    imag_part = center[..., 3:6, :, :, :]
    applied = jnp.concatenate(
        [
            image[..., 0:3, :, :, :] + mass_real * real_part - mass_imag * imag_part,
            image[..., 3:6, :, :, :] + mass_real * imag_part + mass_imag * real_part,
        ],
        axis=-4,
    )
    residual = source - applied
    diagonal = 4.0 + mass_real
    return (center + weight * residual / diagonal) * inside[1:-1][:, None, None]


def edge_parts(adjoint, saved):
    saved_wide = saved.astype(jnp.float32)
    moment = (
        saved_wide[..., 0:3, :, :, :] * adjoint[..., 3:6, :, :, :]
        + saved_wide[..., 3:6, :, :, :] * adjoint[..., 0:3, :, :, :]
    )
    moment_x = moment[..., 0, :, :, :]
    moment_y = moment[..., 1, :, :, :]
    moment_z = moment[..., 2, :, :, :]
    part_x = moment_x + ahead_depth(moment_x)
    part_x = part_x + ahead_rows(part_x)
    part_y = moment_y + ahead_depth(moment_y)
    part_z = moment_z + ahead_rows(moment_z)
    return (part_x, part_y, part_z)


def transposed_smooth(summed, rough):
    rows_in = summed.shape[-2]
    depth_in = summed.shape[-1]
    total = jnp.zeros_like(summed)
    for vertical in range(3):
        for lateral in range(3):
            product = rough[vertical * 3 + lateral] * summed
            padded = jnp.pad(product, ((0, 0), (1, 1), (1, 1)))
            total = (
                total
                + padded[
                    :, 2 - vertical : 2 - vertical + rows_in, 2 - lateral : 2 - lateral + depth_in
                ]
            )
    return total


def inside_mask(first, margin, planes, whole):
    position = first - margin + lax.iota(jnp.int32, planes + 2 * margin)
    return ((position >= 0) & (position < whole)).astype(jnp.float32)


def shards(adjoint_source, forward_field, medium, plane_map, depth, rough):
    planes = adjoint_source.shape[2]
    rows_all = adjoint_source.shape[3]
    depth_all = adjoint_source.shape[4]
    count = lax.axis_size("space")
    index = lax.axis_index("space")
    first = index * planes
    whole = planes * count
    margin = SWEEPS - 1
    joined = jnp.concatenate([adjoint_source, medium[None]], axis=1)
    widened = padded_2(joined, (("space", 2),), margin)
    source_wide = widened[:, 0:6]
    real_wide = widened[:, 6:7]
    imag_wide = widened[:, 7:8]
    inside_wide = inside_mask(first, margin, planes, whole)
    extent = planes + 2 * margin
    adjoint = sweep_steps[0] * source_wide / (4.0 + real_wide)
    for sweep_index in range(1, SWEEPS):
        stop = extent - sweep_index
        adjoint = sweep(
            adjoint,
            source_wide[:, :, sweep_index:stop],
            real_wide[:, :, sweep_index:stop],
            imag_wide[:, :, sweep_index:stop],
            inside_wide[sweep_index - 1 : stop + 1],
            sweep_steps[sweep_index],
        )
    part_x, part_y, part_z = edge_parts(adjoint, forward_field)
    next_y, next_z = shifted((part_y[..., :1, :, :], part_z[..., :1, :, :]), "space", -1)
    shifted_y = jnp.concatenate([part_y[..., 1:, :, :], next_y], axis=-3)
    shifted_z = jnp.concatenate([part_z[..., 1:, :, :], next_z], axis=-3)
    cell = 0.25 * (part_x + (part_y + shifted_y) + (part_z + shifted_z))
    keep = (lax.iota(jnp.int32, depth_all)[None, None, None, :] < depth[..., None]).astype(
        jnp.float32
    )
    local = jnp.sum(cell * keep, axis=0)
    offsets = plane_map - index
    targets = lax.iota(jnp.int32, 2 * REACH + 1) - REACH
    select = (offsets[None] == targets[:, None, None]).astype(jnp.float32)
    window = jnp.einsum("oxy,xyz->oyz", select, local, precision=lax.Precision.HIGHEST)
    window = jnp.sum(window.reshape(2 * REACH + 1, rows_all // 2, 2, depth_all), axis=2)
    owned = window[REACH]
    for offset in range(-REACH, REACH + 1):
        if offset != 0:
            owned = owned + shifted(window[REACH + offset], "space", offset)
    total = over_copies(owned, "src")
    return transposed_smooth(total[None], rough)


def solution(mesh):
    in_specs = (
        P("src", None, "space", None, None),
        P("src", None, "space", None, None),
        P(None, "space", None, None),
        P("space", None),
        P("src", "space", None),
        P(None, "space", None, None),
    )
    out_specs = P("space", None, None)
    return jax.shard_map(shards, mesh=mesh, in_specs=in_specs, out_specs=out_specs, check_vma=False)
```

profile of v0, /device:TPU:24, one launch (start us, length us, event | category | flops | bytes accessed | tf_op | source)
XLA Modules:
  0.0 79.4 jit_solution(15374171242286348099)
XLA Ops:
  0.0 2.4 %fusion.9 = (f32[1,8,3,64,128]{4,3,2,1,0:T(8,128)}, f32[1,8,3,64,128]{4,3,2,1,0:T(8,128)S(1)}) fusion(f32[1,6,4,64,128]{4,3,2,1,0:T(8,128)} %param.6, f32[1,2,4,64,128]{4,3,2,1,0:T(8,128)} %bitcast.157), kind=kLoop, calls=%fused_computation.17 | loop fusion | flops 393216 | bytes 2621440 | tf_op jit(solution)/shard_map/concatenate | solution.py:163
  2.4 2.0 %collective-permute-start = (f32[1,8,3,64,128]{4,3,2,1,0:T(8,128)}, f32[1,8,3,64,128]{4,3,2,1,0:T(8,128)S(1)}, u32[]{:S(2)}, u32[]{:S(2)}) collective-permute-start(f32[1,8,3,64,128]{4,3,2,1,0:T(8,128)} %get-tuple-element.26), channel_id=1, source_target_pairs={{0,1},{1,2},{2,3},{3,4},{4,5},{5,6},{6,7},{7,8},{8,9},{9,10},{10,1... | collective-permute-start | bytes 2359304 | tf_op jit(solution)/shard_map/ppermute | solution.py:20
  4.5 18.3 %collective-permute-start.1 = (f32[1,8,3,64,128]{4,3,2,1,0:T(8,128)S(1)}, f32[1,8,3,64,128]{4,3,2,1,0:T(8,128)S(1)}, u32[]{:S(2)}, u32[]{:S(2)}) collective-permute-start(f32[1,8,3,64,128]{4,3,2,1,0:T(8,128)S(1)} %get-tuple-element.27), channel_id=1, source_target_pairs={{1,0},{2,1},{3,2},{4,3},{5,4},{6,5},{7,6},{8,7},{9,8},{10,9},{11,1... | collective-permute-start | bytes 2359304 | tf_op jit(solution)/shard_map/ppermute | solution.py:21
  23.2 1.1 %convert_element_type.18 = f32[1,6,4,64,128]{4,3,2,1,0:T(8,128)S(1)} convert(bf16[1,6,4,64,128]{4,3,2,1,0:T(8,128)(2,1)} %param.7) | non-fusion elementwise | flops 196608 | bytes 1179648 | tf_op jit(solution)/shard_map/convert_element_type | solution.py:117
  24.3 6.4 %collective-permute-done = f32[1,8,3,64,128]{4,3,2,1,0:T(8,128)S(1)} collective-permute-done((f32[1,8,3,64,128]{4,3,2,1,0:T(8,128)}, f32[1,8,3,64,128]{4,3,2,1,0:T(8,128)S(1)}, u32[]{:S(2)}, u32[]{:S(2)}) %collective-permute-start) | collective-permute-done | bytes 786464 | tf_op jit(solution)/shard_map/ppermute | solution.py:20
  30.7 1.5 %collective-permute-done.1 = f32[1,8,3,64,128]{4,3,2,1,0:T(8,128)S(1)} collective-permute-done((f32[1,8,3,64,128]{4,3,2,1,0:T(8,128)S(1)}, f32[1,8,3,64,128]{4,3,2,1,0:T(8,128)S(1)}, u32[]{:S(2)}, u32[]{:S(2)}) %collective-permute-start.1) | collective-permute-done | bytes 786464 | tf_op jit(solution)/shard_map/ppermute | solution.py:21
  32.5 0.4 fusion
  33.0 0.2 slice.623
  33.4 0.2 slice.638
  33.6 0.6 fusion.18
  34.4 0.5 subtract_bitcast_fusion
  35.2 0.4 fusion.12
  35.6 0.6 fusion.4
  36.8 0.5 fusion.26
  37.4 0.4 subtract_bitcast_fusion.1
  38.0 0.3 fusion.16
  38.3 0.4 fusion.8
  39.2 0.3 fusion.37
  39.7 0.3 subtract_bitcast_fusion.2
  40.2 0.3 fusion.10
  41.0 6.1 %collective-permute-start.2 = (f32[1,1,64,128]{3,2,1,0:T(8,128)S(1)}, f32[1,1,64,128]{3,2,1,0:T(8,128)S(1)}, u32[]{:S(2)}, u32[]{:S(2)}) collective-permute-start(f32[1,1,64,128]{3,2,1,0:T(8,128)S(1)} %slice.711), channel_id=1, source_target_pairs={{1,0},{2,1},{3,2},{4,3},{5,4},{6,5},{7,6},{8,7},{9,8},{10,9},{11,1... | collective-permute-start | bytes 98312 | tf_op jit(solution)/shard_map/ppermute | solution.py:29
  47.1 1.9 %collective-permute-start.3 = (f32[1,1,64,128]{3,2,1,0:T(8,128)S(1)}, f32[1,1,64,128]{3,2,1,0:T(8,128)S(1)}, u32[]{:S(2)}, u32[]{:S(2)}) collective-permute-start(f32[1,1,64,128]{3,2,1,0:T(8,128)S(1)} %slice.715), channel_id=1, source_target_pairs={{1,0},{2,1},{3,2},{4,3},{5,4},{6,5},{7,6},{8,7},{9,8},{10,9},{11,1... | collective-permute-start | bytes 98312 | tf_op jit(solution)/shard_map/ppermute | solution.py:29
  49.2 1.4 %collective-permute-done.3 = f32[1,1,64,128]{3,2,1,0:T(8,128)S(1)} collective-permute-done((f32[1,1,64,128]{3,2,1,0:T(8,128)S(1)}, f32[1,1,64,128]{3,2,1,0:T(8,128)S(1)}, u32[]{:S(2)}, u32[]{:S(2)}) %collective-permute-start.3) | collective-permute-done | bytes 32800 | tf_op jit(solution)/shard_map/ppermute | solution.py:29
  50.7 0.6 bitcast_reduce_fusion
  51.4 2.1 %collective-permute-start.4 = (f32[32,128]{1,0:T(8,128)S(1)}, f32[32,128]{1,0:T(8,128)S(1)}, u32[]{:S(2)}, u32[]{:S(2)}) collective-permute-start(f32[32,128]{1,0:T(8,128)S(1)} %bitcast.171), channel_id=1, source_target_pairs={{2,0},{3,1},{4,2},{5,3},{6,4},{7,5},{8,6},{9,7},{10,8},{11,9},{12,... | collective-permute-start | bytes 49160 | tf_op jit(solution)/shard_map/ppermute | solution.py:29
  53.5 5.6 %collective-permute-start.5 = (f32[32,128]{1,0:T(8,128)S(1)}, f32[32,128]{1,0:T(8,128)S(1)}, u32[]{:S(2)}, u32[]{:S(2)}) collective-permute-start(f32[32,128]{1,0:T(8,128)S(1)} %bitcast.170), channel_id=1, source_target_pairs={{1,0},{2,1},{3,2},{4,3},{5,4},{6,5},{7,6},{8,7},{9,8},{10,9},{11,1... | collective-permute-start | bytes 49160 | tf_op jit(solution)/shard_map/ppermute | solution.py:29
  59.1 2.0 %collective-permute-start.6 = (f32[32,128]{1,0:T(8,128)S(1)}, f32[32,128]{1,0:T(8,128)S(1)}, u32[]{:S(2)}, u32[]{:S(2)}) collective-permute-start(f32[32,128]{1,0:T(8,128)S(1)} %bitcast.169), channel_id=1, source_target_pairs={{0,1},{1,2},{2,3},{3,4},{4,5},{5,6},{6,7},{7,8},{8,9},{9,10},{10,1... | collective-permute-start | bytes 49160 | tf_op jit(solution)/shard_map/ppermute | solution.py:29
  61.1 3.5 %collective-permute-start.7 = (f32[32,128]{1,0:T(8,128)S(1)}, f32[32,128]{1,0:T(8,128)S(1)}, u32[]{:S(2)}, u32[]{:S(2)}) collective-permute-start(f32[32,128]{1,0:T(8,128)S(1)} %bitcast.168), channel_id=1, source_target_pairs={{0,2},{1,3},{2,4},{3,5},{4,6},{5,7},{6,8},{7,9},{8,10},{9,11},{10,... | collective-permute-start | bytes 49160 | tf_op jit(solution)/shard_map/ppermute | solution.py:29
  64.7 1.6 %collective-permute-done.6 = f32[32,128]{1,0:T(8,128)S(1)} collective-permute-done((f32[32,128]{1,0:T(8,128)S(1)}, f32[32,128]{1,0:T(8,128)S(1)}, u32[]{:S(2)}, u32[]{:S(2)}) %collective-permute-start.6) | collective-permute-done | bytes 16416 | tf_op jit(solution)/shard_map/ppermute | solution.py:29
  66.3 2.6 %collective-permute-done.7 = f32[32,128]{1,0:T(8,128)S(1)} collective-permute-done((f32[32,128]{1,0:T(8,128)S(1)}, f32[32,128]{1,0:T(8,128)S(1)}, u32[]{:S(2)}, u32[]{:S(2)}) %collective-permute-start.7) | collective-permute-done | bytes 16416 | tf_op jit(solution)/shard_map/ppermute | solution.py:29
  68.9 9.7 %all_to_all.5 = f32[4,32,128]{2,1,0:T(8,128)S(1)} all-to-all(f32[4,32,128]{2,1,0:T(8,128)S(1)} %broadcast_in_dim.5), channel_id=1, replica_groups=mesh['src'=4,'space'=256] {'src'}, dimensions={0} | all-to-all | bytes 131072 | tf_op jit(solution)/shard_map/all_to_all | solution.py:34
  78.6 0.7 fusion.64
  (73 shorter events, 3.6 us)
Async XLA Ops:
  0.0 24.2 %copy-start.4 = (s32[4,64]{1,0:T(4,128)S(1)}, s32[4,64]{1,0:T(4,128)}, u32[]{:S(2)}) copy-start(s32[4,64]{1,0:T(4,128)} %param.9) | copy-start | bytes 3076
  0.0 24.3 %copy-start.1 = (f32[2,4,64,128]{3,2,1,0:T(8,128)S(1)}, f32[2,4,64,128]{3,2,1,0:T(8,128)}, u32[]{:S(2)}) copy-start(f32[2,4,64,128]{3,2,1,0:T(8,128)} %param.8) | copy-start | bytes 786436
  2.4 29.8 %copy-start = (f32[1,6,4,64,128]{4,3,2,1,0:T(8,128)S(1)}, f32[1,6,4,64,128]{4,3,2,1,0:T(8,128)}, u32[]{:S(2)}) copy-start(f32[1,6,4,64,128]{4,3,2,1,0:T(8,128)} %param.6) | copy-start | bytes 2359300
  2.4 28.3 %collective-permute-start = (f32[1,8,3,64,128]{4,3,2,1,0:T(8,128)}, f32[1,8,3,64,128]{4,3,2,1,0:T(8,128)S(1)}, u32[]{:S(2)}, u32[]{:S(2)}) collective-permute-start(f32[1,8,3,64,128]{4,3,2,1,0:T(8,128)} %get-tuple-element.26), channel_id=1, source_target_pairs={{0,1},{1,2},{2,3},{3,4},{4,5},{5,6},{6,7},{7,8},{8,9},{9,10},{10,1... | collective-permute-start | bytes 2359304 | tf_op jit(solution)/shard_map/ppermute | solution.py:20
  4.5 27.8 %collective-permute-start.1 = (f32[1,8,3,64,128]{4,3,2,1,0:T(8,128)S(1)}, f32[1,8,3,64,128]{4,3,2,1,0:T(8,128)S(1)}, u32[]{:S(2)}, u32[]{:S(2)}) collective-permute-start(f32[1,8,3,64,128]{4,3,2,1,0:T(8,128)S(1)} %get-tuple-element.27), channel_id=1, source_target_pairs={{1,0},{2,1},{3,2},{4,3},{5,4},{6,5},{7,6},{8,7},{9,8},{10,9},{11,1... | collective-permute-start | bytes 2359304 | tf_op jit(solution)/shard_map/ppermute | solution.py:21
  40.7 9.9 %copy-start.3 = (s32[1,4,64]{2,1,0:T(4,128)S(1)}, s32[1,4,64]{2,1,0:T(4,128)}, u32[]{:S(2)}) copy-start(s32[1,4,64]{2,1,0:T(4,128)} %param.10) | copy-start | bytes 3076
  41.0 37.7 %copy-start.2 = (f32[9,1,32,128]{3,2,1,0:T(8,128)S(1)}, f32[9,1,32,128]{3,2,1,0:T(8,128)}, u32[]{:S(2)}) copy-start(f32[9,1,32,128]{3,2,1,0:T(8,128)} %param.11) | copy-start | bytes 442372
  41.0 8.2 %collective-permute-start.2 = (f32[1,1,64,128]{3,2,1,0:T(8,128)S(1)}, f32[1,1,64,128]{3,2,1,0:T(8,128)S(1)}, u32[]{:S(2)}, u32[]{:S(2)}) collective-permute-start(f32[1,1,64,128]{3,2,1,0:T(8,128)S(1)} %slice.711), channel_id=1, source_target_pairs={{1,0},{2,1},{3,2},{4,3},{5,4},{6,5},{7,6},{8,7},{9,8},{10,9},{11,1... | collective-permute-start | bytes 98312 | tf_op jit(solution)/shard_map/ppermute | solution.py:29
  47.1 3.5 %collective-permute-start.3 = (f32[1,1,64,128]{3,2,1,0:T(8,128)S(1)}, f32[1,1,64,128]{3,2,1,0:T(8,128)S(1)}, u32[]{:S(2)}, u32[]{:S(2)}) collective-permute-start(f32[1,1,64,128]{3,2,1,0:T(8,128)S(1)} %slice.715), channel_id=1, source_target_pairs={{1,0},{2,1},{3,2},{4,3},{5,4},{6,5},{7,6},{8,7},{9,8},{10,9},{11,1... | collective-permute-start | bytes 98312 | tf_op jit(solution)/shard_map/ppermute | solution.py:29
  51.4 13.3 %collective-permute-start.4 = (f32[32,128]{1,0:T(8,128)S(1)}, f32[32,128]{1,0:T(8,128)S(1)}, u32[]{:S(2)}, u32[]{:S(2)}) collective-permute-start(f32[32,128]{1,0:T(8,128)S(1)} %bitcast.171), channel_id=1, source_target_pairs={{2,0},{3,1},{4,2},{5,3},{6,4},{7,5},{8,6},{9,7},{10,8},{11,9},{12,... | collective-permute-start | bytes 49160 | tf_op jit(solution)/shard_map/ppermute | solution.py:29
  53.5 11.2 %collective-permute-start.5 = (f32[32,128]{1,0:T(8,128)S(1)}, f32[32,128]{1,0:T(8,128)S(1)}, u32[]{:S(2)}, u32[]{:S(2)}) collective-permute-start(f32[32,128]{1,0:T(8,128)S(1)} %bitcast.170), channel_id=1, source_target_pairs={{1,0},{2,1},{3,2},{4,3},{5,4},{6,5},{7,6},{8,7},{9,8},{10,9},{11,1... | collective-permute-start | bytes 49160 | tf_op jit(solution)/shard_map/ppermute | solution.py:29
  59.1 7.2 %collective-permute-start.6 = (f32[32,128]{1,0:T(8,128)S(1)}, f32[32,128]{1,0:T(8,128)S(1)}, u32[]{:S(2)}, u32[]{:S(2)}) collective-permute-start(f32[32,128]{1,0:T(8,128)S(1)} %bitcast.169), channel_id=1, source_target_pairs={{0,1},{1,2},{2,3},{3,4},{4,5},{5,6},{6,7},{7,8},{8,9},{9,10},{10,1... | collective-permute-start | bytes 49160 | tf_op jit(solution)/shard_map/ppermute | solution.py:29
  61.1 7.7 %collective-permute-start.7 = (f32[32,128]{1,0:T(8,128)S(1)}, f32[32,128]{1,0:T(8,128)S(1)}, u32[]{:S(2)}, u32[]{:S(2)}) collective-permute-start(f32[32,128]{1,0:T(8,128)S(1)} %bitcast.168), channel_id=1, source_target_pairs={{0,2},{1,3},{2,4},{3,5},{4,6},{5,7},{6,8},{7,9},{8,10},{9,11},{10,... | collective-permute-start | bytes 49160 | tf_op jit(solution)/shard_map/ppermute | solution.py:29
where the time goes:
time: 79.8 us; the launch traced here: 79.4 us
  starting transfers between devices  41.6 us (52%)
  waiting for transfers between devices  13.6 us (17%)
  other arithmetic  10.4 us (13%)
  blocking collectives  9.72 us (12%)
  local copies, waits for them, and re-layouts  2.84 us (4%)
    ppermute x6, starting transfers between devices, shifted(): lax.ppermute(value, axis, [(source, source + steps) for source in range(f...  21.2 us
    ppermute x1, starting transfers between devices, padded_2(): after = lax.ppermute(first, axis, down)  18.3 us
    all_to_all x1, blocking collectives, from_everyone(): return lax.all_to_all(copies, axis, split_axis=0, concat_axis=0, tiled=True)  9.72 us
    ppermute x1, waiting for transfers between devices, padded_2(): before = lax.ppermute(last, axis, up)  6.42 us
    ppermute x6, waiting for transfers between devices, shifted(): lax.ppermute(value, axis, [(source, source + steps) for source in range(f...  5.59 us
    concatenate x1, other arithmetic, shards(): joined = jnp.concatenate([adjoint_source, medium[None]], axis=1)  2.41 us
    ppermute x1, starting transfers between devices, padded_2(): before = lax.ppermute(last, axis, up)  2.04 us
  transfers between devices with their start and end apart: 8, of which 5 were waited for; matrix products, arithmetic and copies ran while one was open for 2% of the time, Pallas kernels for 0%

commit v1 on v0

v1 whole, which is shorter than its diff:
```python
import functools

import jax
import jax.numpy as jnp
from jax import lax
from jax.experimental import pallas as pl
from jax.experimental.pallas import tpu as pltpu
from jax.sharding import PartitionSpec as P

MESH = pl.DeviceIdType.MESH
SWEEPS = 4
REACH = 2
STEPS = (0.323, 1.658, 0.422, 0.752)
PAD = 8
BLOCK = 16
LOW, HIGH = -REACH - 1, REACH


def kernel(
    groups, count,
    source_hbm, saved_hbm, medium_hbm, map_hbm, depth_hbm, rough_hbm,
    out_ref,
    source, saved, mass, plane_map, depth, rough,
    inverse, field, mixed, part, upper, lower, where_to, how_deep, edge_out, edge_in,
    window, sent, landed, total, shares, padded,
    source_sem, mass_sem, load_sem, halo_send, halo_recv, edge_sem, window_send, window_recv, share_send, share_recv,
):
    planes, rows, cells = source.shape[1:]
    group = lax.axis_index("src")
    me = lax.axis_index("space")
    core = lax.rem(me, 2)
    has_below, has_above = me > 0, me < count - 1
    blocks = range(0, rows, BLOCK)
    lane = lax.broadcasted_iota(jnp.int32, (BLOCK, cells), 1)
    first_lane, last_lane = lane == 0, lane == cells - 1

    def at(start):
        return pl.ds(PAD + start, BLOCK)

    def ahead(value):
        return jnp.where(last_lane, 0.0, pltpu.roll(value, cells - 1, 1))

    def behind(value):
        return jnp.where(first_lane, 0.0, pltpu.roll(value, 1, 1))

    def present(offset):
        other = me + offset
        return (other >= 0) & (other < count)

    barrier = pltpu.get_barrier_semaphore()
    awaited = groups - 1
    for offset in (1, -1, 2, -2, 3):
        @pl.when(present(offset))
        def _():
            pl.semaphore_signal(barrier, inc=1, device_id={"space": me + offset}, device_id_type=MESH)
    for offset in range(1, groups):
        pl.semaphore_signal(barrier, inc=1, device_id={"src": lax.rem(group + offset, groups)}, device_id_type=MESH)
    for offset in range(LOW, HIGH + 1):
        if offset != 0:
            awaited = awaited + present(offset).astype(jnp.int32)

    def load_source(p):
        return pltpu.make_async_copy(source_hbm.at[0, :, p], source.at[:, p], source_sem.at[p])

    def load_mass(p):
        return pltpu.make_async_copy(medium_hbm.at[:, p], mass.at[:, p], mass_sem.at[p])

    for p in (0, planes - 1, *range(1, planes - 1)):
        load_source(p).start()
        load_mass(p).start()
    load_depth = pltpu.make_async_copy(depth_hbm.at[0], depth, load_sem.at[0])
    load_map = pltpu.make_async_copy(map_hbm, plane_map, load_sem.at[1])
    load_saved = pltpu.make_async_copy(saved_hbm.at[0], saved, load_sem.at[2])
    load_rough = pltpu.make_async_copy(rough_hbm.at[:, 0], rough, load_sem.at[3])
    for load in (load_depth, load_map, load_saved, load_rough):
        load.start()

    margin = jnp.zeros((PAD, cells), jnp.float32)
    for k in range(SWEEPS - 1):
        for p in range(planes):
            for c in (0, 1, 4, 5):
                field[k, p, c, pl.ds(PAD + rows, PAD), :] = margin
            for c in (2, 3):
                field[k, p + 1, c, pl.ds(0, PAD), :] = margin
                mixed[k, p + 1, c, pl.ds(0, PAD), :] = margin
            for c in (4, 5):
                mixed[k, p + 1, c, pl.ds(0, PAD), :] = margin
    for c in (0, 1):
        part[c, pl.ds(PAD + rows, PAD), :] = margin
    padded[...] = jnp.zeros_like(padded)

    @pl.when(jnp.logical_not(has_below))
    def _():
        for k in range(SWEEPS - 1):
            mixed[k, 0] = jnp.zeros(mixed.shape[2:], jnp.float32)
        edge_in[...] = jnp.full(edge_in.shape, -1000.0, jnp.float32)

    @pl.when(jnp.logical_not(has_above))
    def _():
        for k in range(SWEEPS - 1):
            field[k, planes, 2:6] = jnp.zeros((4, *field.shape[3:]), jnp.float32)

    def halo_down(k):
        return pltpu.make_async_remote_copy(
            src_ref=field.at[k, 0, 2:6, PAD:PAD + rows],
            dst_ref=field.at[k, planes, 2:6, PAD:PAD + rows],
            send_sem=halo_send.at[k, 0],
            recv_sem=halo_recv.at[k, 0],
            device_id={"space": me - 1},
            device_id_type=MESH,
        )

    def halo_up(k):
        return pltpu.make_async_remote_copy(
            src_ref=mixed.at[k, planes, 0:4, PAD:PAD + rows],
            dst_ref=mixed.at[k, 0, 0:4, PAD:PAD + rows],
            send_sem=halo_send.at[k, 1],
            recv_sem=halo_recv.at[k, 1],
            device_id={"space": me + 1},
            device_id_type=MESH,
        )

    edge_up = pltpu.make_async_remote_copy(
        src_ref=edge_out,
        dst_ref=edge_in,
        send_sem=edge_sem.at[0],
        recv_sem=edge_sem.at[1],
        device_id={"space": me + 1},
        device_id_type=MESH,
    )

    def combine(k, p):
        for r in blocks:
            for i in (0, 1):
                x, y, z = (field[k, p, 2 * c + i, at(r), :] for c in range(3))
                x_next, z_next = (field[k, p, 2 * c + i, at(r + 1), :] for c in (0, 2))
                mixed[k, p + 1, i, at(r), :] = (ahead(x) - x) + z
                mixed[k, p + 1, 2 + i, at(r), :] = y + (x_next - x)
                mixed[k, p + 1, 4 + i, at(r), :] = (z_next - z) - (ahead(y) - y)

    def begin(p):
        load_source(p).wait()
        load_mass(p).wait()
        for r in blocks:
            span = pl.ds(r, BLOCK)
            turned = 1.0 / (4.0 + mass[0, p, span, :])
            inverse[p, span, :] = turned
            turned = STEPS[0] * turned
            for c in range(3):
                for i in (0, 1):
                    field[0, p, 2 * c + i, at(r), :] = source[c + 3 * i, p, span, :] * turned
        combine(0, p)

    def update(k, p, weight):
        before = k - 1
        inside = jnp.where((me == 0) & (p == 0), 0.0, 1.0).astype(jnp.float32)
        for r in blocks:
            span = pl.ds(r, BLOCK)
            real, imag = mass[0, p, span, :], mass[1, p, span, :]
            scale = weight * inverse[p, span, :]
            images, centers = [], []
            for i in (0, 1):
                x, y, z = (field[before, p, 2 * c + i, at(r), :] for c in range(3))
                y_up = field[before, p + 1, 2 + i, at(r), :]
                z_up = field[before, p + 1, 4 + i, at(r), :]
                curl_x = mixed[before, p + 1, 4 + i, at(r), :]
                curl_y = mixed[before, p + 1, i, at(r), :] - z_up
                curl_z = y_up - mixed[before, p + 1, 2 + i, at(r), :]
                curl_x_left = mixed[before, p + 1, 4 + i, at(r - 1), :]
                curl_z_left = field[before, p + 1, 2 + i, at(r - 1), :] - mixed[before, p + 1, 2 + i, at(r - 1), :]
                curl_y_low = (mixed[before, p, i, at(r), :] - z) * inside
                curl_z_low = (y - mixed[before, p, 2 + i, at(r), :]) * inside
                images.append((
                    (behind(curl_y) - curl_y) - (curl_z_left - curl_z),
                    (curl_z_low - curl_z) - (behind(curl_x) - curl_x),
                    (curl_x_left - curl_x) - (curl_y_low - curl_y),
                ))
                centers.append((x, y, z))
            for c in range(3):
                e_r, e_i = centers[0][c], centers[1][c]
                res_r = source[c, p, span, :] - (images[0][c] + real * e_r - imag * e_i)
                res_i = source[c + 3, p, span, :] - (images[1][c] + real * e_i + imag * e_r)
                field[k, p, 2 * c, at(r), :] = e_r + scale * res_r
                field[k, p, 2 * c + 1, at(r), :] = e_i + scale * res_i

    def moments(p):
        for r in blocks:
            span = pl.ds(r, BLOCK)
            m = []
            for c in range(3):
                f_r = saved[c, p, span, :].astype(jnp.float32)
                f_i = saved[c + 3, p, span, :].astype(jnp.float32)
                a_r = field[SWEEPS - 1, p, 2 * c, at(r), :]
                a_i = field[SWEEPS - 1, p, 2 * c + 1, at(r), :]
                m.append(0.25 * (f_r * a_i + f_i * a_r))
            part[0, at(r), :] = m[0] + ahead(m[0])
            part[1, at(r), :] = m[2]
            lower[p, span, :] = m[1] + ahead(m[1])
        for r in blocks:
            span = pl.ds(r, BLOCK)
            shared = lower[p, span, :] + (part[1, at(r), :] + part[1, at(r + 1), :])
            lower[p, span, :] = shared
            upper[p, span, :] = shared + (part[0, at(r), :] + part[0, at(r + 1), :])

    def outer(t, carry):
        begin(jnp.where(t == core, 0, planes - 1))
        return carry

    lax.fori_loop(0, 2, outer, 0)
    pl.semaphore_wait(barrier, awaited)

    @pl.when(has_below)
    def _():
        halo_down(0).start()

    @pl.when(has_above)
    def _():
        halo_up(0).start()

    def inner(p, carry):
        begin(p)
        return carry

    lax.fori_loop(1, planes - 1, inner, 0)

    load_depth.wait()
    load_map.wait()
    edge_out[...] = jnp.zeros_like(edge_out)
    edge_out[0:1, 0:rows] = depth[planes - 1:planes, :].astype(jnp.float32)
    edge_out[1:2, 0:rows] = plane_map[planes - 1:planes, :].astype(jnp.float32)

    @pl.when(has_above)
    def _():
        edge_up.start()

    diagonal = lax.broadcasted_iota(jnp.int32, (rows, rows), 0) == lax.broadcasted_iota(jnp.int32, (rows, rows), 1)

    def columns(row):
        spread = jnp.where(diagonal, jnp.broadcast_to(row, (rows, rows)), 0.0)
        return jnp.broadcast_to(jnp.sum(spread, axis=1, keepdims=True), (rows, cells))

    for p in range(planes):
        how_deep[p] = columns(depth[p:p + 1, :].astype(jnp.float32))
        where_to[p] = columns(plane_map[p:p + 1, :].astype(jnp.float32))

    def turn(n, carry):
        k = n // planes + 1
        t = lax.rem(n, planes)
        outermost = t >= planes - 2
        p = jnp.where(outermost, jnp.where((t == planes - 2) == (core == 0), planes - 1, 0), t + 1)
        weight = jnp.where(k == 1, STEPS[1], jnp.where(k == 2, STEPS[2], STEPS[3])).astype(jnp.float32)

        @pl.when((p == 0) & has_below)
        def _():
            halo_up(k - 1).wait_recv()

        @pl.when((p == planes - 1) & has_above)
        def _():
            halo_down(k - 1).wait_recv()

        update(k, p, weight)

        @pl.when(k < SWEEPS - 1)
        def _():
            @pl.when((p == 0) & has_below)
            def _():
                halo_down(k).start()

            combine(k, p)

            @pl.when((p == planes - 1) & has_above)
            def _():
                halo_up(k).start()

        @pl.when(k == SWEEPS - 1)
        def _():
            @pl.when(t == 0)
            def _():
                load_saved.wait()

            moments(p)

        return carry

    lax.fori_loop(0, (SWEEPS - 1) * planes, turn, 0)

    @pl.when(has_above)
    def _():
        edge_up.wait_send()

    @pl.when(has_below)
    def _():
        edge_up.wait_recv()

    how_deep[planes] = columns(edge_in[0:1, 0:rows])
    where_to[planes] = columns(edge_in[1:2, 0:rows])

    place = lane.astype(jnp.float32)
    origin = me.astype(jnp.float32)
    for r in blocks:
        span = pl.ds(r, BLOCK)
        kept, targets = [], []
        for p in range(planes + 1):
            if p == planes:
                value = lower[0, span, :]
            elif p == planes - 1:
                value = upper[p, span, :]
            else:
                value = upper[p, span, :] + lower[p + 1, span, :]
            kept.append(jnp.where(place < how_deep[p, span, :], value, 0.0))
            targets.append(where_to[p, span, :] - origin)
        for offset in range(LOW, HIGH + 1):
            sum_here = jnp.zeros((BLOCK, cells), jnp.float32)
            for p in range(planes + 1):
                if (p == planes and offset < HIGH) or (p < planes and offset > LOW):
                    sum_here = sum_here + jnp.where(targets[p] == float(offset), kept[p], 0.0)
            window[offset - LOW, span, :] = sum_here

    halves = rows // 2
    sizes = range(HIGH - LOW + 1)
    def window_copy(slot):
        return pltpu.make_async_remote_copy(
            src_ref=sent.at[slot],
            dst_ref=landed.at[slot],
            send_sem=window_send.at[slot],
            recv_sem=window_recv.at[slot],
            device_id={"space": me + (slot + LOW)},
            device_id_type=MESH,
        )

    for slot in sizes:
        folded = window[slot, pl.ds(0, halves, stride=2), :] + window[slot, pl.ds(1, halves, stride=2), :]
        if slot + LOW == 0:
            total[...] = folded
        else:
            sent[slot] = folded

            @pl.when(present(slot + LOW))
            def _():
                window_copy(slot).start()

    for slot in sizes:
        if slot + LOW != 0:
            @pl.when(present(-(slot + LOW)))
            def _():
                window_copy(slot).wait_recv()
                total[...] += landed[slot]

    shares[group] = total[...]
    def share_copy(offset):
        return pltpu.make_async_remote_copy(
            src_ref=shares.at[group],
            dst_ref=shares.at[group],
            send_sem=share_send.at[offset - 1],
            recv_sem=share_recv.at[offset - 1],
            device_id={"src": lax.rem(group + offset, groups)},
            device_id_type=MESH,
        )

    def share_from(offset):
        slot = lax.rem(group + groups - offset, groups)
        return pltpu.make_async_remote_copy(
            src_ref=shares.at[slot],
            dst_ref=shares.at[slot],
            send_sem=share_send.at[offset - 1],
            recv_sem=share_recv.at[offset - 1],
            device_id={"src": lax.rem(group + offset, groups)},
            device_id_type=MESH,
        )

    for offset in range(1, groups):
        share_copy(offset).start()
    load_rough.wait()
    for offset in range(1, groups):
        share_from(offset).wait_recv()
    whole = shares[0]
    for slot in range(1, groups):
        whole = whole + shares[slot]

    lanes = lax.broadcasted_iota(jnp.int32, (halves, cells), 1)
    for a in range(3):
        left, middle, right = (rough[3 * a + b] * whole for b in range(3))
        row_sum = middle
        row_sum = row_sum + jnp.where(lanes == cells - 1, 0.0, pltpu.roll(left, cells - 1, 1))
        row_sum = row_sum + jnp.where(lanes == 0, 0.0, pltpu.roll(right, 1, 1))
        padded[a, pl.ds(PAD, halves), :] = row_sum
    out_ref[0] = (
        padded[1, pl.ds(PAD, halves), :]
        + padded[0, pl.ds(PAD + 1, halves), :]
        + padded[2, pl.ds(PAD - 1, halves), :]
    )

    for k in range(SWEEPS - 1):
        @pl.when(has_below)
        def _():
            halo_down(k).wait_send()

        @pl.when(has_above)
        def _():
            halo_up(k).wait_send()
    for slot in sizes:
        if slot + LOW != 0:
            @pl.when(present(slot + LOW))
            def _():
                window_copy(slot).wait_send()
    for offset in range(1, groups):
        share_copy(offset).wait_send()


def solution(mesh):
    groups, count = mesh.shape["src"], mesh.shape["space"]

    def step(adjoint_source, forward_field, medium, plane_map, depth, rough):
        parts, planes, rows, cells = adjoint_source.shape[1:]
        halves = rows // 2
        tall = rows + 2 * PAD
        slots = HIGH - LOW + 1
        f32 = jnp.float32
        dma = pltpu.SemaphoreType.DMA
        return pl.pallas_call(
            functools.partial(kernel, groups, count),
            out_shape=jax.ShapeDtypeStruct((1, halves, cells), f32),
            in_specs=[pl.BlockSpec(memory_space=pl.ANY)] * 6,
            out_specs=pl.BlockSpec(memory_space=pltpu.VMEM),
            scratch_shapes=[
                pltpu.VMEM((parts, planes, rows, cells), f32),
                pltpu.VMEM((parts, planes, rows, cells), jnp.bfloat16),
                pltpu.VMEM((2, planes, rows, cells), f32),
                pltpu.VMEM((planes, rows), jnp.int32),
                pltpu.VMEM((planes, rows), jnp.int32),
                pltpu.VMEM((9, halves, cells), f32),
                pltpu.VMEM((planes, rows, cells), f32),
                pltpu.VMEM((SWEEPS, planes + 1, 6, tall, cells), f32),
                pltpu.VMEM((SWEEPS - 1, planes + 1, 6, tall, cells), f32),
                pltpu.VMEM((2, tall, cells), f32),
                pltpu.VMEM((planes, rows, cells), f32),
                pltpu.VMEM((planes, rows, cells), f32),
                pltpu.VMEM((planes + 1, rows, cells), f32),
                pltpu.VMEM((planes + 1, rows, cells), f32),
                pltpu.VMEM((8, 128), f32),
                pltpu.VMEM((8, 128), f32),
                pltpu.VMEM((slots, rows, cells), f32),
                pltpu.VMEM((slots, halves, cells), f32),
                pltpu.VMEM((slots, halves, cells), f32),
                pltpu.VMEM((halves, cells), f32),
                pltpu.VMEM((groups, halves, cells), f32),
                pltpu.VMEM((3, halves + 2 * PAD, cells), f32),
                dma((planes,)),
                dma((planes,)),
                dma((4,)),
                dma((SWEEPS - 1, 2)),
                dma((SWEEPS - 1, 2)),
                dma((2,)),
                dma((slots,)),
                dma((slots,)),
                dma((groups - 1,)),
                dma((groups - 1,)),
            ],
            compiler_params=pltpu.CompilerParams(
                collective_id=0, has_side_effects=True, vmem_limit_bytes=62 * 1024 * 1024
            ),
            name="gradient",
        )(adjoint_source, forward_field, medium, plane_map, depth, rough)

    in_specs = (
        P("src", None, "space", None, None),
        P("src", None, "space", None, None),
        P(None, "space", None, None),
        P("space", None),
        P("src", "space", None),
        P(None, "space", None, None),
    )
    out_specs = P("space", None, None)
    return jax.shard_map(step, mesh=mesh, in_specs=in_specs, out_specs=out_specs, check_vma=False)
```

time: 79.8 us -> 43.1 us (0.54)
  Pallas kernels: 0 us -> 41.6 us
  starting transfers between devices: 41.6 us -> 0 us
  waiting for transfers between devices: 13.6 us -> 0 us
  other arithmetic: 10.4 us -> 0 us
  blocking collectives: 9.72 us -> 0 us
  local copies, waits for them, and re-layouts: 2.84 us -> 1.32 us
    ppermute x8 -> x0, starting transfers between devices: 41.6 us -> none  [the longest x6 21.2 us: shifted(): lax.ppermute(value, axis, [(source, source + steps) for source in range(f...]
    pallas_call x0 -> x1, Pallas kernels: none -> 41.6 us  [step(): pl.pallas_call(functools.partial(kernel, groups, count), out_shape=jax.Sh...]
    ppermute x8 -> x0, waiting for transfers between devices: 13.6 us -> none  [the longest x1 6.42 us: padded_2(): before = lax.ppermute(last, axis, up)]
    all_to_all x1 -> x0, blocking collectives: 9.72 us -> none  [from_everyone(): return lax.all_to_all(copies, axis, split_axis=0, concat_axis=0, tiled=True)]
    mul x7 -> x0, other arithmetic: 2.79 us -> none  [the longest x3 1.41 us: curl_curl(): curl_z = curl_z * front]
    concatenate x2 -> x0, other arithmetic: 2.59 us -> none  [the longest x1 2.41 us: shards(): joined = jnp.concatenate([adjoint_source, medium[None]], axis=1)]
    slice x38 -> x0, local copies, waits for them, and re-layouts: 2.35 us -> none  [the longest x8 1.27 us: ahead_depth(): value[..., 1:]]
    another operation x6 -> x0, other arithmetic: 1.56 us -> none  [curl_curl(): stacked = jnp.stack([out_x, out_y, out_z], axis=-4)]
  transfers between devices with their start and end apart: 8 -> 0, of which waited for: 5 -> 0; matrix products, arithmetic and copies ran while one was open for 2% -> 0% of each run, Pallas kernels for 0% -> 0%
where the time goes in v1:
time: 43.1 us; the launch traced here: 42.9 us
  Pallas kernels  41.6 us (97%)
  local copies, waits for them, and re-layouts  1.32 us (3%)
    pallas_call x1, Pallas kernels, step(): pl.pallas_call(functools.partial(kernel, groups, count), out_shape=jax.Sh...  41.6 us
    unnamed x1, local copies, waits for them, and re-layouts  1.32 us

profile of v1, /device:TPU:24, one launch (start us, length us, event | category | flops | bytes accessed | tf_op | source)
XLA Modules:
  0.0 42.9 jit_solution(15318146445050907478)
XLA Ops:
  0.0 41.6 %gradient.1 = f32[1,32,128]{2,1,0:T(8,128)} custom-call(f32[1,6,4,64,128]{4,3,2,1,0:T(8,128)} %source_hbm.1, bf16[1,6,4,64,128]{4,3,2,1,0:T(8,128)(2,1)} %saved_hbm.1, f32[2,4,64,128]{3,2,1,0:T(8,128)} %medium_hbm.1, s32[4,64]{1,0:T(4,128)} %map_hbm.1, s32[1,4,64]{2,1,0:T(4,128)} %depth_hbm.1, f32[9,1,32,128]{3,2,1,0:T(8,128)} %rough_hbm.1), custom_call_target="tpu_custom_call" | custom-call | tf_op jit(solution)/shard_map/gradient/pallas_call | solution.py:420
  41.6 1.3 %copy.8 = f32[1,32,128]{2,1,0:T(8,128)} copy(f32[1,32,128]{2,1,0:T(8,128)} %gradient.1) | data formatting | bytes 32768

commit v2 on v1

--- a/solution.py
+++ b/solution.py
@@ -13,6 +13,7 @@
 STEPS = (0.323, 1.658, 0.422, 0.752)
 PAD = 8
 BLOCK = 16
+PIECES = 4
 LOW, HIGH = -REACH - 1, REACH
 
 
@@ -85,8 +86,9 @@
                 mixed[k, p + 1, c, pl.ds(0, PAD), :] = margin
             for c in (4, 5):
                 mixed[k, p + 1, c, pl.ds(0, PAD), :] = margin
-    for c in (0, 1):
-        part[c, pl.ds(PAD + rows, PAD), :] = margin
+    for p in range(planes):
+        for c in (0, 1):
+            part[p, c, pl.ds(PAD + rows, PAD), :] = margin
     padded[...] = jnp.zeros_like(padded)
 
     @pl.when(jnp.logical_not(has_below))
@@ -100,22 +102,27 @@
         for k in range(SWEEPS - 1):
             field[k, planes, 2:6] = jnp.zeros((4, *field.shape[3:]), jnp.float32)
 
-    def halo_down(k):
+    piece = rows // PIECES
+
+    def rows_of(q):
+        return pl.ds(PAD + q * piece, piece)
+
+    def halo_down(k, q):
         return pltpu.make_async_remote_copy(
-            src_ref=field.at[k, 0, 2:6, PAD:PAD + rows],
-            dst_ref=field.at[k, planes, 2:6, PAD:PAD + rows],
-            send_sem=halo_send.at[k, 0],
-            recv_sem=halo_recv.at[k, 0],
+            src_ref=field.at[k, 0, 2:6, rows_of(q)],
+            dst_ref=field.at[k, planes, 2:6, rows_of(q)],
+            send_sem=halo_send.at[k, 0, q],
+            recv_sem=halo_recv.at[k, 0, q],
             device_id={"space": me - 1},
             device_id_type=MESH,
         )
 
-    def halo_up(k):
+    def halo_up(k, q):
         return pltpu.make_async_remote_copy(
-            src_ref=mixed.at[k, planes, 0:4, PAD:PAD + rows],
-            dst_ref=mixed.at[k, 0, 0:4, PAD:PAD + rows],
-            send_sem=halo_send.at[k, 1],
-            recv_sem=halo_recv.at[k, 1],
+            src_ref=mixed.at[k, planes, 0:4, rows_of(q)],
+            dst_ref=mixed.at[k, 0, 0:4, rows_of(q)],
+            send_sem=halo_send.at[k, 1, q],
+            recv_sem=halo_recv.at[k, 1, q],
             device_id={"space": me + 1},
             device_id_type=MESH,
         )
@@ -129,8 +136,8 @@
         device_id_type=MESH,
     )
 
-    def combine(k, p):
-        for r in blocks:
+    def combine(k, p, span=blocks):
+        for r in span:
             for i in (0, 1):
                 x, y, z = (field[k, p, 2 * c + i, at(r), :] for c in range(3))
                 x_next, z_next = (field[k, p, 2 * c + i, at(r + 1), :] for c in (0, 2))
@@ -151,10 +158,10 @@
                     field[0, p, 2 * c + i, at(r), :] = source[c + 3 * i, p, span, :] * turned
         combine(0, p)
 
-    def update(k, p, weight):
+    def update(k, p, weight, span_of=blocks):
         before = k - 1
         inside = jnp.where((me == 0) & (p == 0), 0.0, 1.0).astype(jnp.float32)
-        for r in blocks:
+        for r in span_of:
             span = pl.ds(r, BLOCK)
             real, imag = mass[0, p, span, :], mass[1, p, span, :]
             scale = weight * inverse[p, span, :]
@@ -183,8 +190,8 @@
                 field[k, p, 2 * c, at(r), :] = e_r + scale * res_r
                 field[k, p, 2 * c + 1, at(r), :] = e_i + scale * res_i
 
-    def moments(p):
-        for r in blocks:
+    def products(p, span_of=blocks):
+        for r in span_of:
             span = pl.ds(r, BLOCK)
             m = []
             for c in range(3):
@@ -193,111 +200,23 @@
                 a_r = field[SWEEPS - 1, p, 2 * c, at(r), :]
                 a_i = field[SWEEPS - 1, p, 2 * c + 1, at(r), :]
                 m.append(0.25 * (f_r * a_i + f_i * a_r))
-            part[0, at(r), :] = m[0] + ahead(m[0])
-            part[1, at(r), :] = m[2]
+            part[p, 0, at(r), :] = m[0] + ahead(m[0])
+            part[p, 1, at(r), :] = m[2]
             lower[p, span, :] = m[1] + ahead(m[1])
-        for r in blocks:
+
+    def averages(p, span_of=blocks):
+        for r in span_of:
             span = pl.ds(r, BLOCK)
-            shared = lower[p, span, :] + (part[1, at(r), :] + part[1, at(r + 1), :])
+            shared = lower[p, span, :] + (part[p, 1, at(r), :] + part[p, 1, at(r + 1), :])
             lower[p, span, :] = shared
-            upper[p, span, :] = shared + (part[0, at(r), :] + part[0, at(r + 1), :])
-
-    def outer(t, carry):
-        begin(jnp.where(t == core, 0, planes - 1))
-        return carry
-
-    lax.fori_loop(0, 2, outer, 0)
-    pl.semaphore_wait(barrier, awaited)
-
-    @pl.when(has_below)
-    def _():
-        halo_down(0).start()
-
-    @pl.when(has_above)
-    def _():
-        halo_up(0).start()
-
-    def inner(p, carry):
-        begin(p)
-        return carry
-
-    lax.fori_loop(1, planes - 1, inner, 0)
-
-    load_depth.wait()
-    load_map.wait()
-    edge_out[...] = jnp.zeros_like(edge_out)
-    edge_out[0:1, 0:rows] = depth[planes - 1:planes, :].astype(jnp.float32)
-    edge_out[1:2, 0:rows] = plane_map[planes - 1:planes, :].astype(jnp.float32)
-
-    @pl.when(has_above)
-    def _():
-        edge_up.start()
-
-    diagonal = lax.broadcasted_iota(jnp.int32, (rows, rows), 0) == lax.broadcasted_iota(jnp.int32, (rows, rows), 1)
-
-    def columns(row):
-        spread = jnp.where(diagonal, jnp.broadcast_to(row, (rows, rows)), 0.0)
-        return jnp.broadcast_to(jnp.sum(spread, axis=1, keepdims=True), (rows, cells))
-
-    for p in range(planes):
-        how_deep[p] = columns(depth[p:p + 1, :].astype(jnp.float32))
-        where_to[p] = columns(plane_map[p:p + 1, :].astype(jnp.float32))
-
-    def turn(n, carry):
-        k = n // planes + 1
-        t = lax.rem(n, planes)
-        outermost = t >= planes - 2
-        p = jnp.where(outermost, jnp.where((t == planes - 2) == (core == 0), planes - 1, 0), t + 1)
-        weight = jnp.where(k == 1, STEPS[1], jnp.where(k == 2, STEPS[2], STEPS[3])).astype(jnp.float32)
-
-        @pl.when((p == 0) & has_below)
-        def _():
-            halo_up(k - 1).wait_recv()
-
-        @pl.when((p == planes - 1) & has_above)
-        def _():
-            halo_down(k - 1).wait_recv()
-
-        update(k, p, weight)
-
-        @pl.when(k < SWEEPS - 1)
-        def _():
-            @pl.when((p == 0) & has_below)
-            def _():
-                halo_down(k).start()
-
-            combine(k, p)
-
-            @pl.when((p == planes - 1) & has_above)
-            def _():
-                halo_up(k).start()
-
-        @pl.when(k == SWEEPS - 1)
-        def _():
-            @pl.when(t == 0)
-            def _():
-                load_saved.wait()
-
-            moments(p)
-
-        return carry
-
-    lax.fori_loop(0, (SWEEPS - 1) * planes, turn, 0)
-
-    @pl.when(has_above)
-    def _():
-        edge_up.wait_send()
-
-    @pl.when(has_below)
-    def _():
-        edge_up.wait_recv()
-
-    how_deep[planes] = columns(edge_in[0:1, 0:rows])
-    where_to[planes] = columns(edge_in[1:2, 0:rows])
+            upper[p, span, :] = shared + (part[p, 0, at(r), :] + part[p, 0, at(r + 1), :])
 
     place = lane.astype(jnp.float32)
     origin = me.astype(jnp.float32)
-    for r in blocks:
+    halves = rows // 2
+    slots = range(HIGH - LOW + 1)
+
+    def window_sums(r):
         span = pl.ds(r, BLOCK)
         kept, targets = [], []
         for p in range(planes + 1):
@@ -309,15 +228,148 @@
                 value = upper[p, span, :] + lower[p + 1, span, :]
             kept.append(jnp.where(place < how_deep[p, span, :], value, 0.0))
             targets.append(where_to[p, span, :] - origin)
-        for offset in range(LOW, HIGH + 1):
+        for slot in slots:
+            offset = slot + LOW
+            terms = [p for p in range(planes + 1) if (p == planes and offset < HIGH) or (p < planes and offset > LOW)]
             sum_here = jnp.zeros((BLOCK, cells), jnp.float32)
-            for p in range(planes + 1):
-                if (p == planes and offset < HIGH) or (p < planes and offset > LOW):
-                    sum_here = sum_here + jnp.where(targets[p] == float(offset), kept[p], 0.0)
-            window[offset - LOW, span, :] = sum_here
-
-    halves = rows // 2
-    sizes = range(HIGH - LOW + 1)
+            for p in terms:
+                sum_here = sum_here + jnp.where(targets[p] == float(offset), kept[p], 0.0)
+            window[slot, span, :] = sum_here
+            folded = window[slot, pl.ds(r, BLOCK // 2, stride=2), :] + window[slot, pl.ds(r + 1, BLOCK // 2, stride=2), :]
+            sent[slot, pl.ds(r // 2, BLOCK // 2), :] = folded
+
+    def outer(t, carry):
+        begin(jnp.where(t == core, 0, planes - 1))
+        return carry
+
+    lax.fori_loop(0, 2, outer, 0)
+    pl.semaphore_wait(barrier, awaited)
+
+    @pl.when(has_below)
+    def _():
+        for q in range(PIECES):
+            halo_down(0, q).start()
+
+    @pl.when(has_above)
+    def _():
+        for q in range(PIECES):
+            halo_up(0, q).start()
+
+    def inner(p, carry):
+        begin(p)
+        return carry
+
+    lax.fori_loop(1, planes - 1, inner, 0)
+
+    load_depth.wait()
+    load_map.wait()
+    edge_out[...] = jnp.zeros_like(edge_out)
+    edge_out[0:1, 0:rows] = depth[planes - 1:planes, :].astype(jnp.float32)
+    edge_out[1:2, 0:rows] = plane_map[planes - 1:planes, :].astype(jnp.float32)
+
+    @pl.when(has_above)
+    def _():
+        edge_up.start()
+
+    diagonal = lax.broadcasted_iota(jnp.int32, (rows, rows), 0) == lax.broadcasted_iota(jnp.int32, (rows, rows), 1)
+
+    def columns(row):
+        spread = jnp.where(diagonal, jnp.broadcast_to(row, (rows, rows)), 0.0)
+        return jnp.broadcast_to(jnp.sum(spread, axis=1, keepdims=True), (rows, cells))
+
+    for p in range(planes):
+        how_deep[p] = columns(depth[p:p + 1, :].astype(jnp.float32))
+        where_to[p] = columns(plane_map[p:p + 1, :].astype(jnp.float32))
+
+    def await_halo(k, p, q):
+        @pl.when((p == 0) & has_below)
+        def _():
+            halo_up(k, q).wait_recv()
+
+        @pl.when((p == planes - 1) & has_above)
+        def _():
+            halo_down(k, q).wait_recv()
+
+    def blocks_of(q):
+        return range(q * piece, (q + 1) * piece, BLOCK)
+
+    def end_at(t):
+        return jnp.where(t == core, planes - 1, 0)
+
+    def complete_after(q):
+        return [q - 1] * (q > 0) + [q] * (q == PIECES - 1)
+
+    def turn(k, carry):
+        weight = jnp.where(k == 1, STEPS[1], STEPS[2]).astype(jnp.float32)
+
+        def middle(p, carry):
+            update(k, p, weight)
+            combine(k, p)
+            return carry
+
+        lax.fori_loop(1, planes - 1, middle, 0)
+
+        for q in range(PIECES):
+            def ends(t, carry):
+                p = end_at(t)
+                await_halo(k - 1, p, q)
+                update(k, p, weight, blocks_of(q))
+
+                @pl.when((p == 0) & has_below)
+                def _():
+                    halo_down(k, q).start()
+
+                for ready in complete_after(q):
+                    combine(k, p, blocks_of(ready))
+
+                    @pl.when((p == planes - 1) & has_above)
+                    def _():
+                        halo_up(k, ready).start()
+
+                return carry
+
+            lax.fori_loop(0, 2, ends, 0)
+        return carry
+
+    lax.fori_loop(1, SWEEPS - 1, turn, 0)
+
+    last = SWEEPS - 1
+    load_saved.wait()
+
+    def middle(p, carry):
+        update(last, p, STEPS[last])
+        products(p)
+        averages(p)
+        return carry
+
+    lax.fori_loop(1, planes - 1, middle, 0)
+
+    @pl.when(has_above)
+    def _():
+        edge_up.wait_send()
+
+    @pl.when(has_below)
+    def _():
+        edge_up.wait_recv()
+
+    how_deep[planes] = columns(edge_in[0:1, 0:rows])
+    where_to[planes] = columns(edge_in[1:2, 0:rows])
+
+    for q in range(PIECES):
+        def ends(t, carry):
+            p = end_at(t)
+            await_halo(last - 1, p, q)
+            update(last, p, STEPS[last], blocks_of(q))
+            products(p, blocks_of(q))
+            for ready in complete_after(q):
+                averages(p, blocks_of(ready))
+            return carry
+
+        lax.fori_loop(0, 2, ends, 0)
+        for ready in complete_after(q):
+            for r in blocks_of(ready):
+                window_sums(r)
+
     def window_copy(slot):
         return pltpu.make_async_remote_copy(
             src_ref=sent.at[slot],
@@ -328,18 +380,14 @@
             device_id_type=MESH,
         )
 
-    for slot in sizes:
-        folded = window[slot, pl.ds(0, halves, stride=2), :] + window[slot, pl.ds(1, halves, stride=2), :]
-        if slot + LOW == 0:
-            total[...] = folded
-        else:
-            sent[slot] = folded
-
+    for slot in sorted(slots, key=lambda slot: -abs(slot + LOW)):
+        if slot + LOW != 0:
             @pl.when(present(slot + LOW))
             def _():
                 window_copy(slot).start()
 
-    for slot in sizes:
+    total[...] = sent[-LOW]
+    for slot in slots:
         if slot + LOW != 0:
             @pl.when(present(-(slot + LOW)))
             def _():
@@ -368,8 +416,24 @@
             device_id_type=MESH,
         )
 
-    for offset in range(1, groups):
+    for offset in sorted(range(1, groups), key=lambda offset: -min(offset, groups - offset)):
         share_copy(offset).start()
+
+    for k in range(SWEEPS - 1):
+        @pl.when(has_below)
+        def _():
+            for q in range(PIECES):
+                halo_down(k, q).wait_send()
+
+        @pl.when(has_above)
+        def _():
+            for q in range(PIECES):
+                halo_up(k, q).wait_send()
+    for slot in slots:
+        if slot + LOW != 0:
+            @pl.when(present(slot + LOW))
+            def _():
+                window_copy(slot).wait_send()
     load_rough.wait()
     for offset in range(1, groups):
         share_from(offset).wait_recv()
@@ -390,19 +454,6 @@
         + padded[2, pl.ds(PAD - 1, halves), :]
     )
 
-    for k in range(SWEEPS - 1):
-        @pl.when(has_below)
-        def _():
-            halo_down(k).wait_send()
-
-        @pl.when(has_above)
-        def _():
-            halo_up(k).wait_send()
-    for slot in sizes:
-        if slot + LOW != 0:
-            @pl.when(present(slot + LOW))
-            def _():
-                window_copy(slot).wait_send()
     for offset in range(1, groups):
         share_copy(offset).wait_send()
 
@@ -420,7 +471,7 @@
         return pl.pallas_call(
             functools.partial(kernel, groups, count),
             out_shape=jax.ShapeDtypeStruct((1, halves, cells), f32),
-            in_specs=[pl.BlockSpec(memory_space=pl.ANY)] * 6,
+            in_specs=[pl.BlockSpec(memory_space=pltpu.HBM)] * 6,
             out_specs=pl.BlockSpec(memory_space=pltpu.VMEM),
             scratch_shapes=[
                 pltpu.VMEM((parts, planes, rows, cells), f32),
@@ -432,7 +483,7 @@
                 pltpu.VMEM((planes, rows, cells), f32),
                 pltpu.VMEM((SWEEPS, planes + 1, 6, tall, cells), f32),
                 pltpu.VMEM((SWEEPS - 1, planes + 1, 6, tall, cells), f32),
-                pltpu.VMEM((2, tall, cells), f32),
+                pltpu.VMEM((planes, 2, tall, cells), f32),
                 pltpu.VMEM((planes, rows, cells), f32),
                 pltpu.VMEM((planes, rows, cells), f32),
                 pltpu.VMEM((planes + 1, rows, cells), f32),
@@ -448,8 +499,8 @@
                 dma((planes,)),
                 dma((planes,)),
                 dma((4,)),
-                dma((SWEEPS - 1, 2)),
-                dma((SWEEPS - 1, 2)),
+                dma((SWEEPS - 1, 2, PIECES)),
+                dma((SWEEPS - 1, 2, PIECES)),
                 dma((2,)),
                 dma((slots,)),
                 dma((slots,)),
@@ -457,10 +508,10 @@
                 dma((groups - 1,)),
             ],
             compiler_params=pltpu.CompilerParams(
-                collective_id=0, has_side_effects=True, vmem_limit_bytes=62 * 1024 * 1024
+                collective_id=0, has_side_effects=True, vmem_limit_bytes=48 * 1024 * 1024
             ),
             name="gradient",
-        )(adjoint_source, forward_field, medium, plane_map, depth, rough)
+        )(*(pltpu.with_memory_space_constraint(given, pltpu.HBM) for given in (adjoint_source, forward_field, medium, plane_map, depth, rough)))
 
     in_specs = (
         P("src", None, "space", None, None),

time: 43.1 us -> 40.3 us (0.935)
  Pallas kernels: 41.6 us -> 39.5 us
  local copies, waits for them, and re-layouts: 1.32 us -> 0.61 us
    pallas_call x1, Pallas kernels: 41.6 us -> 39.5 us  [step(): pl.pallas_call(functools.partial(kernel, groups, count), out_shape=jax.Sh...]
    unnamed x1, local copies, waits for them, and re-layouts: 1.32 us -> 0.61 us
where the time goes in v2:
time: 40.3 us; the launch traced here: 40.1 us
  Pallas kernels  39.5 us (98%)
  local copies, waits for them, and re-layouts  0.61 us (2%)
    pallas_call x1, Pallas kernels, step(): pl.pallas_call(functools.partial(kernel, groups, count), out_shape=jax.Sh...  39.5 us

profile of v2, /device:TPU:24, one launch (start us, length us, event | category | flops | bytes accessed | tf_op | source)
XLA Modules:
  0.0 40.1 jit_solution(10554257077218867816)
XLA Ops:
  0.0 39.5 %gradient.1 = f32[1,32,128]{2,1,0:T(8,128)S(1)} custom-call(f32[1,6,4,64,128]{4,3,2,1,0:T(8,128)} %source_hbm.1, bf16[1,6,4,64,128]{4,3,2,1,0:T(8,128)(2,1)} %saved_hbm.1, f32[2,4,64,128]{3,2,1,0:T(8,128)} %medium_hbm.1, s32[4,64]{1,0:T(4,128)} %map_hbm.1, s32[1,4,64]{2,1,0:T(4,128)} %depth_hbm.1, f32[9,1,32,128]{3,2,1,0:T(8,128)} %rough_hbm.1), custom_call_target="tpu_custom_call" | custom-call | tf_op jit(solution)/shard_map/gradient/pallas_call | solution.py:471
  39.5 0.6 %copy.8 = f32[1,32,128]{2,1,0:T(8,128)} copy(f32[1,32,128]{2,1,0:T(8,128)S(1)} %gradient.1) | data formatting | bytes 32768

commit v3 on v2

--- a/solution.py
+++ b/solution.py
@@ -48,17 +48,25 @@
         other = me + offset
         return (other >= 0) & (other < count)
 
+    across = 1 - 2 * core
+    even = core == 0
+
     barrier = pltpu.get_barrier_semaphore()
-    awaited = groups - 1
-    for offset in (1, -1, 2, -2, 3):
+    for low, high in ((1, 1), (-1, -1), (2, 2), (3, -2), (4, -3)):
+        offset = jnp.where(even, low, high)
+
         @pl.when(present(offset))
         def _():
             pl.semaphore_signal(barrier, inc=1, device_id={"space": me + offset}, device_id_type=MESH)
     for offset in range(1, groups):
-        pl.semaphore_signal(barrier, inc=1, device_id={"src": lax.rem(group + offset, groups)}, device_id_type=MESH)
-    for offset in range(LOW, HIGH + 1):
-        if offset != 0:
-            awaited = awaited + present(offset).astype(jnp.int32)
+        pl.semaphore_signal(
+            barrier, inc=1,
+            device_id={"src": lax.rem(group + offset, groups), "space": me + across},
+            device_id_type=MESH,
+        )
+    awaited = groups - 1
+    for low, high in ((1, 1), (-1, -1), (-2, -2), (-4, 2), (3, -3)):
+        awaited = awaited + present(jnp.where(even, low, high)).astype(jnp.int32)
 
     def load_source(p):
         return pltpu.make_async_copy(source_hbm.at[0, :, p], source.at[:, p], source_sem.at[p])
@@ -245,14 +253,13 @@
     lax.fori_loop(0, 2, outer, 0)
     pl.semaphore_wait(barrier, awaited)
 
-    @pl.when(has_below)
-    def _():
-        for q in range(PIECES):
+    for q in range(PIECES):
+        @pl.when(has_below)
+        def _():
             halo_down(0, q).start()
 
-    @pl.when(has_above)
-    def _():
-        for q in range(PIECES):
+        @pl.when(has_above)
+        def _():
             halo_up(0, q).start()
 
     def inner(p, carry):
@@ -371,52 +378,58 @@
                 window_sums(r)
 
     def window_copy(slot):
+        offset = slot + LOW
         return pltpu.make_async_remote_copy(
             src_ref=sent.at[slot],
             dst_ref=landed.at[slot],
             send_sem=window_send.at[slot],
             recv_sem=window_recv.at[slot],
-            device_id={"space": me + (slot + LOW)},
+            device_id={"space": me + offset + (across if offset % 2 == 0 else -across)},
             device_id_type=MESH,
         )
 
-    for slot in sorted(slots, key=lambda slot: -abs(slot + LOW)):
-        if slot + LOW != 0:
-            @pl.when(present(slot + LOW))
-            def _():
-                window_copy(slot).start()
-
-    total[...] = sent[-LOW]
-    for slot in slots:
-        if slot + LOW != 0:
-            @pl.when(present(-(slot + LOW)))
-            def _():
-                window_copy(slot).wait_recv()
-                total[...] += landed[slot]
-
-    shares[group] = total[...]
+    def leaves(slot):
+        offset = slot + LOW
+        return present(offset) & (offset != across)
+
+    def lands(slot):
+        offset = slot + LOW
+        return present(across - offset) & (offset != across)
+
+    farthest_first = sorted(slots, key=lambda slot: -abs(slot + LOW))
+    for slot in farthest_first:
+        @pl.when(leaves(slot))
+        def _():
+            window_copy(slot).start()
+
+    total[...] = sent[across - LOW]
+    for slot in farthest_first[::-1]:
+        @pl.when(lands(slot))
+        def _():
+            window_copy(slot).wait_recv()
+            total[...] += landed[slot]
+
     def share_copy(offset):
         return pltpu.make_async_remote_copy(
-            src_ref=shares.at[group],
+            src_ref=total,
             dst_ref=shares.at[group],
-            send_sem=share_send.at[offset - 1],
-            recv_sem=share_recv.at[offset - 1],
-            device_id={"src": lax.rem(group + offset, groups)},
+            send_sem=share_send.at[offset],
+            recv_sem=share_recv.at[offset],
+            device_id={"src": lax.rem(group + offset, groups), "space": me + across},
             device_id_type=MESH,
         )
 
     def share_from(offset):
-        slot = lax.rem(group + groups - offset, groups)
         return pltpu.make_async_remote_copy(
-            src_ref=shares.at[slot],
-            dst_ref=shares.at[slot],
-            send_sem=share_send.at[offset - 1],
-            recv_sem=share_recv.at[offset - 1],
-            device_id={"src": lax.rem(group + offset, groups)},
+            src_ref=total,
+            dst_ref=shares.at[lax.rem(group + groups - offset, groups)],
+            send_sem=share_send.at[offset],
+            recv_sem=share_recv.at[offset],
+            device_id={"src": lax.rem(group + offset, groups), "space": me + across},
             device_id_type=MESH,
         )
 
-    for offset in sorted(range(1, groups), key=lambda offset: -min(offset, groups - offset)):
+    for offset in sorted(range(groups), key=lambda offset: -min(offset, groups - offset)):
         share_copy(offset).start()
 
     for k in range(SWEEPS - 1):
@@ -430,12 +443,11 @@
             for q in range(PIECES):
                 halo_up(k, q).wait_send()
     for slot in slots:
-        if slot + LOW != 0:
-            @pl.when(present(slot + LOW))
-            def _():
-                window_copy(slot).wait_send()
+        @pl.when(leaves(slot))
+        def _():
+            window_copy(slot).wait_send()
     load_rough.wait()
-    for offset in range(1, groups):
+    for offset in range(groups):
         share_from(offset).wait_recv()
     whole = shares[0]
     for slot in range(1, groups):
@@ -454,7 +466,7 @@
         + padded[2, pl.ds(PAD - 1, halves), :]
     )
 
-    for offset in range(1, groups):
+    for offset in range(groups):
         share_copy(offset).wait_send()
 
 
@@ -504,8 +516,8 @@
                 dma((2,)),
                 dma((slots,)),
                 dma((slots,)),
-                dma((groups - 1,)),
-                dma((groups - 1,)),
+                dma((groups,)),
+                dma((groups,)),
             ],
             compiler_params=pltpu.CompilerParams(
                 collective_id=0, has_side_effects=True, vmem_limit_bytes=48 * 1024 * 1024

time: 40.3 us -> 40.6 us (level); the launches traced: 40.1 us -> 39.9 us
  no operation moved by 1% of the time
where the time goes in v3:
time: 40.6 us; the launch traced here: 39.9 us
  Pallas kernels  39.2 us (97%)
  local copies, waits for them, and re-layouts  0.61 us (2%)
    pallas_call x1, Pallas kernels, step(): pl.pallas_call(functools.partial(kernel, groups, count), out_shape=jax.Sh...  39.2 us

profile of v3, /device:TPU:24, one launch (start us, length us, event | category | flops | bytes accessed | tf_op | source)
XLA Modules:
  0.0 39.9 jit_solution(10313228490037084004)
XLA Ops:
  0.0 39.2 %gradient.1 = f32[1,32,128]{2,1,0:T(8,128)S(1)} custom-call(f32[1,6,4,64,128]{4,3,2,1,0:T(8,128)} %source_hbm.1, bf16[1,6,4,64,128]{4,3,2,1,0:T(8,128)(2,1)} %saved_hbm.1, f32[2,4,64,128]{3,2,1,0:T(8,128)} %medium_hbm.1, s32[4,64]{1,0:T(4,128)} %map_hbm.1, s32[1,4,64]{2,1,0:T(4,128)} %depth_hbm.1, f32[9,1,32,128]{3,2,1,0:T(8,128)} %rough_hbm.1), custom_call_target="tpu_custom_call" | custom-call | tf_op jit(solution)/shard_map/gradient/pallas_call | solution.py:483
  39.2 0.6 %copy.8 = f32[1,32,128]{2,1,0:T(8,128)} copy(f32[1,32,128]{2,1,0:T(8,128)S(1)} %gradient.1) | data formatting | bytes 32768

commit v4 on v3

--- a/solution.py
+++ b/solution.py
@@ -253,13 +253,14 @@
     lax.fori_loop(0, 2, outer, 0)
     pl.semaphore_wait(barrier, awaited)
 
-    for q in range(PIECES):
-        @pl.when(has_below)
-        def _():
+    @pl.when(has_below)
+    def _():
+        for q in range(PIECES):
             halo_down(0, q).start()
 
-        @pl.when(has_above)
-        def _():
+    @pl.when(has_above)
+    def _():
+        for q in range(PIECES):
             halo_up(0, q).start()
 
     def inner(p, carry):

time: 40.6 us -> 40.6 us (level)
  no operation moved by 1% of the time
where the time goes in v4:
time: 40.6 us; the launch traced here: 39.9 us
  Pallas kernels  39.2 us (97%)
  local copies, waits for them, and re-layouts  0.61 us (2%)
    pallas_call x1, Pallas kernels, step(): pl.pallas_call(functools.partial(kernel, groups, count), out_shape=jax.Sh...  39.2 us

profile of v4, /device:TPU:24, one launch (start us, length us, event | category | flops | bytes accessed | tf_op | source)
XLA Modules:
  0.0 39.9 jit_solution(10898010700339521324)
XLA Ops:
  0.0 39.2 %gradient.1 = f32[1,32,128]{2,1,0:T(8,128)S(1)} custom-call(f32[1,6,4,64,128]{4,3,2,1,0:T(8,128)} %source_hbm.1, bf16[1,6,4,64,128]{4,3,2,1,0:T(8,128)(2,1)} %saved_hbm.1, f32[2,4,64,128]{3,2,1,0:T(8,128)} %medium_hbm.1, s32[4,64]{1,0:T(4,128)} %map_hbm.1, s32[1,4,64]{2,1,0:T(4,128)} %depth_hbm.1, f32[9,1,32,128]{3,2,1,0:T(8,128)} %rough_hbm.1), custom_call_target="tpu_custom_call" | custom-call | tf_op jit(solution)/shard_map/gradient/pallas_call | solution.py:484
  39.2 0.6 %copy.8 = f32[1,32,128]{2,1,0:T(8,128)} copy(f32[1,32,128]{2,1,0:T(8,128)S(1)} %gradient.1) | data formatting | bytes 32768

commit v5 on v2

--- a/solution.py
+++ b/solution.py
@@ -14,6 +14,7 @@
 PAD = 8
 BLOCK = 16
 PIECES = 4
+PARTS = 1
 LOW, HIGH = -REACH - 1, REACH
 
 
@@ -355,6 +356,21 @@
     how_deep[planes] = columns(edge_in[0:1, 0:rows])
     where_to[planes] = columns(edge_in[1:2, 0:rows])
 
+    share = halves // PARTS
+
+    def lines(h):
+        return pl.ds(h * share, share)
+
+    def window_copy(slot, h):
+        return pltpu.make_async_remote_copy(
+            src_ref=sent.at[slot, lines(h)],
+            dst_ref=landed.at[slot, lines(h)],
+            send_sem=window_send.at[slot, h],
+            recv_sem=window_recv.at[slot, h],
+            device_id={"space": me + (slot + LOW)},
+            device_id_type=MESH,
+        )
+
     for q in range(PIECES):
         def ends(t, carry):
             p = end_at(t)
@@ -369,55 +385,46 @@
         for ready in complete_after(q):
             for r in blocks_of(ready):
                 window_sums(r)
-
-    def window_copy(slot):
+            lines_done = (ready + 1) * piece // 2
+            if lines_done % share == 0:
+                for slot in sorted(slots, key=lambda slot: -abs(slot + LOW)):
+                    if slot + LOW != 0:
+                        @pl.when(present(slot + LOW))
+                        def _():
+                            window_copy(slot, lines_done // share - 1).start()
+
+    def share_copy(offset, h):
         return pltpu.make_async_remote_copy(
-            src_ref=sent.at[slot],
-            dst_ref=landed.at[slot],
-            send_sem=window_send.at[slot],
-            recv_sem=window_recv.at[slot],
-            device_id={"space": me + (slot + LOW)},
-            device_id_type=MESH,
-        )
-
-    for slot in sorted(slots, key=lambda slot: -abs(slot + LOW)):
-        if slot + LOW != 0:
-            @pl.when(present(slot + LOW))
-            def _():
-                window_copy(slot).start()
-
-    total[...] = sent[-LOW]
-    for slot in slots:
-        if slot + LOW != 0:
-            @pl.when(present(-(slot + LOW)))
-            def _():
-                window_copy(slot).wait_recv()
-                total[...] += landed[slot]
-
-    shares[group] = total[...]
-    def share_copy(offset):
-        return pltpu.make_async_remote_copy(
-            src_ref=shares.at[group],
-            dst_ref=shares.at[group],
-            send_sem=share_send.at[offset - 1],
-            recv_sem=share_recv.at[offset - 1],
+            src_ref=shares.at[group, lines(h)],
+            dst_ref=shares.at[group, lines(h)],
+            send_sem=share_send.at[offset - 1, h],
+            recv_sem=share_recv.at[offset - 1, h],
             device_id={"src": lax.rem(group + offset, groups)},
             device_id_type=MESH,
         )
 
-    def share_from(offset):
+    def share_from(offset, h):
         slot = lax.rem(group + groups - offset, groups)
         return pltpu.make_async_remote_copy(
-            src_ref=shares.at[slot],
-            dst_ref=shares.at[slot],
-            send_sem=share_send.at[offset - 1],
-            recv_sem=share_recv.at[offset - 1],
+            src_ref=shares.at[slot, lines(h)],
+            dst_ref=shares.at[slot, lines(h)],
+            send_sem=share_send.at[offset - 1, h],
+            recv_sem=share_recv.at[offset - 1, h],
             device_id={"src": lax.rem(group + offset, groups)},
             device_id_type=MESH,
         )
 
-    for offset in sorted(range(1, groups), key=lambda offset: -min(offset, groups - offset)):
-        share_copy(offset).start()
+    for h in range(PARTS):
+        total[lines(h), :] = sent[-LOW, lines(h), :]
+        for slot in sorted(slots, key=lambda slot: abs(slot + LOW)):
+            if slot + LOW != 0:
+                @pl.when(present(-(slot + LOW)))
+                def _():
+                    window_copy(slot, h).wait_recv()
+                    total[lines(h), :] += landed[slot, lines(h), :]
+        shares[group, lines(h), :] = total[lines(h), :]
+        for offset in sorted(range(1, groups), key=lambda offset: -min(offset, groups - offset)):
+            share_copy(offset, h).start()
 
     for k in range(SWEEPS - 1):
         @pl.when(has_below)
@@ -433,10 +440,12 @@
         if slot + LOW != 0:
             @pl.when(present(slot + LOW))
             def _():
-                window_copy(slot).wait_send()
+                for h in range(PARTS):
+                    window_copy(slot, h).wait_send()
     load_rough.wait()
-    for offset in range(1, groups):
-        share_from(offset).wait_recv()
+    for h in range(PARTS):
+        for offset in range(1, groups):
+            share_from(offset, h).wait_recv()
     whole = shares[0]
     for slot in range(1, groups):
         whole = whole + shares[slot]
@@ -454,8 +463,9 @@
         + padded[2, pl.ds(PAD - 1, halves), :]
     )
 
-    for offset in range(1, groups):
-        share_copy(offset).wait_send()
+    for h in range(PARTS):
+        for offset in range(1, groups):
+            share_copy(offset, h).wait_send()
 
 
 def solution(mesh):
@@ -502,10 +512,10 @@
                 dma((SWEEPS - 1, 2, PIECES)),
                 dma((SWEEPS - 1, 2, PIECES)),
                 dma((2,)),
-                dma((slots,)),
-                dma((slots,)),
-                dma((groups - 1,)),
-                dma((groups - 1,)),
+                dma((slots, PARTS)),
+                dma((slots, PARTS)),
+                dma((groups - 1, PARTS)),
+                dma((groups - 1, PARTS)),
             ],
             compiler_params=pltpu.CompilerParams(
                 collective_id=0, has_side_effects=True, vmem_limit_bytes=48 * 1024 * 1024

time: 40.3 us -> 40.3 us (level)
  no operation moved by 1% of the time
where the time goes in v5:
time: 40.3 us; the launch traced here: 40.1 us
  Pallas kernels  39.5 us (98%)
  local copies, waits for them, and re-layouts  0.61 us (2%)
    pallas_call x1, Pallas kernels, step(): pl.pallas_call(functools.partial(kernel, groups, count), out_shape=jax.Sh...  39.5 us

profile of v5, /device:TPU:24, one launch (start us, length us, event | category | flops | bytes accessed | tf_op | source)
XLA Modules:
  0.0 40.1 jit_solution(6135274838688415838)
XLA Ops:
  0.0 39.5 %gradient.1 = f32[1,32,128]{2,1,0:T(8,128)S(1)} custom-call(f32[1,6,4,64,128]{4,3,2,1,0:T(8,128)} %source_hbm.1, bf16[1,6,4,64,128]{4,3,2,1,0:T(8,128)(2,1)} %saved_hbm.1, f32[2,4,64,128]{3,2,1,0:T(8,128)} %medium_hbm.1, s32[4,64]{1,0:T(4,128)} %map_hbm.1, s32[1,4,64]{2,1,0:T(4,128)} %depth_hbm.1, f32[9,1,32,128]{3,2,1,0:T(8,128)} %rough_hbm.1), custom_call_target="tpu_custom_call" | custom-call | tf_op jit(solution)/shard_map/gradient/pallas_call | solution.py:481
  39.5 0.6 %copy.8 = f32[1,32,128]{2,1,0:T(8,128)} copy(f32[1,32,128]{2,1,0:T(8,128)S(1)} %gradient.1) | data formatting | bytes 32768
